TPU v7x, 32 devices: a whole 2x2x4 slice. The times are simulated.
32 devices in a mesh: clip: 2 (over y), frame: 4 (over z), track: 4 (over x, core).
Axes of the slice: x: 2, y: 2, z: 4, core: 2. Of those that a mesh axis runs over, the one named last changes fastest.
Arguments:
- feature_maps: bfloat16 [8, 4096, 256], P(('clip', 'frame')), parts along dimension 0, may hold values from -6 to 6
- query_frame: int32 [1024], P('clip'), parts along dimension 0, may hold values from 0 to 3
- query_row: int32 [1024], P('clip'), parts along dimension 0, may hold values from 0 to 63
- query_col: int32 [1024], P('clip'), parts along dimension 0, may hold values from 0 to 63
- track_order: int32 [1024], P('clip'), parts along dimension 0, may hold values from 0 to 511, each once
- conv_weight: float32 [16, 9], replicated, may hold values from -2 to 2
- conv_bias: float32 [16], replicated, may hold values from -2 to 2
- head_weight: float32 [16], replicated, may hold values from -2 to 2
- mix_in: bfloat16 [256, 1024], replicated, may hold values from -0.375 to 0.375
- temporal_taps: float32 [3, 1024], replicated, may hold values from -2.5 to 2.5
- mix_gain: float32 [1024], replicated, may hold values from 0.25 to 1.75
- mix_out: bfloat16 [1024, 3], replicated, may hold values from -0.1875 to 0.1875
Outputs:
- estimates: float32 [1024, 3, 4], P(('clip', 'frame', 'track')), parts along dimension 0
There are 2 independent parts, one for each index of `clip`. A program takes and returns all parts, laid end to end along the dimension named above; an argument that names none is the same for every part. Nothing has to cross between parts.
Inputs may be any that keep to these rules, and one draw needn't show every extreme that they name: `track_order`: each track appears in exactly one slot.
All inputs are finite; a program needn't handle non-finite values.
Results may differ from a plain program's by a relative error of at most 0.0053.
Values may be sent and summed in bfloat16 or wider, within the bound.
A program may use at most 64 MiB of HBM per device.

v0:
```python
import math

import jax
import jax.numpy as jnp
from jax import lax
from jax.sharding import PartitionSpec as P

GRID_H = 64
GRID_W = 64


def padded_2(block, sides, width):
    for axis, dim in sides:
        count = lax.axis_size(axis)
        forward = [(i, i + 1) for i in range(count - 1)]
        backward = [(target, source) for source, target in forward]
        low = lax.ppermute(
            lax.slice_in_dim(block, block.shape[dim] - width, None, axis=dim), axis, forward
        )
        high = lax.ppermute(lax.slice_in_dim(block, 0, width, axis=dim), axis, backward)
        block = jnp.concatenate([low, block, high], axis=dim)
    return block


def conv_logits(cost, conv_weight, conv_bias, head_weight):
    height, width = (cost.shape[1], cost.shape[2])
    padded = jnp.pad(cost, ((0, 0), (1, 1), (1, 1)))
    logit = jnp.zeros(cost.shape, jnp.float32)
    for channel in range(conv_weight.shape[0]):
        acc = jnp.zeros(cost.shape, jnp.float32) + conv_bias[channel]
        for tap in range(9):
            acc = (
                acc
                + conv_weight[channel, tap]
                * padded[:, tap // 3 : tap // 3 + height, tap % 3 : tap % 3 + width]
            )
        logit = logit + head_weight[channel] * jax.nn.relu(acc)
    return logit


def block_terms(qblock, maps, conv_weight, conv_bias, head_weight, row_pos, col_pos):
    cost = lax.dot_general(
        qblock, maps, (((1,), (1,)), ((), ())), preferred_element_type=jnp.float32
    )
    cost = cost * (1.0 / math.sqrt(maps.shape[1]))
    logit = conv_logits(
        cost.reshape(cost.shape[0], GRID_H, GRID_W), conv_weight, conv_bias, head_weight
    )
    heat = jax.nn.softmax(logit.reshape(cost.shape), axis=-1)
    row_est = jnp.sum(heat * row_pos, axis=-1).astype(jnp.bfloat16)
    col_est = jnp.sum(heat * col_pos, axis=-1).astype(jnp.bfloat16)
    sampled = jnp.dot(heat.astype(jnp.bfloat16), maps, preferred_element_type=jnp.float32).astype(
        jnp.bfloat16
    )
    return (sampled, row_est, col_est)


def temporal_mix(extended, temporal_taps, mix_gain, mix_out):
    mixed = (
        temporal_taps[0] * extended[:, :-2]
        + temporal_taps[1] * extended[:, 1:-1]
        + temporal_taps[2] * extended[:, 2:]
    )
    normed = mixed * lax.rsqrt(jnp.mean(mixed * mixed, axis=-1, keepdims=True) + 1e-06) * mix_gain
    hidden = jax.nn.gelu(normed).astype(jnp.bfloat16)
    rows, frames_here = (hidden.shape[0], hidden.shape[1])
    delta = jnp.dot(
        hidden.reshape(rows * frames_here, hidden.shape[2]),
        mix_out,
        preferred_element_type=jnp.float32,
    )
    return delta.reshape(rows, frames_here, 3)


def assemble(row_est, col_est, delta):
    return jnp.stack(
        [
            row_est.astype(jnp.float32) + delta[:, :, 0],
            col_est.astype(jnp.float32) + delta[:, :, 1],
            delta[:, :, 2],
        ],
        axis=1,
    )


def project(sampled, mix_in):
    rows, frames_here, chan = sampled.shape
    projected = jnp.dot(
        sampled.reshape(rows * frames_here, chan), mix_in, preferred_element_type=jnp.float32
    )
    return projected.reshape(rows, frames_here, mix_in.shape[1])


def on_device(
    feature_maps,
    query_frame,
    query_row,
    query_col,
    track_order,
    conv_weight,
    conv_bias,
    head_weight,
    mix_in,
    temporal_taps,
    mix_gain,
    mix_out,
):
    frame_count = lax.axis_size("frame")
    track_count = lax.axis_size("track")
    frame_here = lax.axis_index("frame")
    track_here = lax.axis_index("track")
    f_dev, pixels, chan = feature_maps.shape
    total = track_order.shape[0]
    tr_dev = total // track_count
    sub_rows = tr_dev // frame_count
    slots = (
        jnp.arange(frame_count, dtype=jnp.int32)[:, None] * track_count + track_here
    ) * sub_rows
    slots = (slots + jnp.arange(sub_rows, dtype=jnp.int32)[None, :]).reshape(tr_dev)
    tracks = track_order[slots]
    local_frame = query_frame[tracks] - frame_here * f_dev
    owned = (local_frame >= 0) & (local_frame < f_dev)
    pixel_ids = query_row[tracks] * GRID_W + query_col[tracks]
    flat = jnp.clip(local_frame, 0, f_dev - 1) * pixels + pixel_ids
    picks = feature_maps.reshape(f_dev * pixels, chan)[flat]
    partial_value = jnp.where(owned[:, None], picks, jnp.zeros((), picks.dtype))
    queries = lax.psum(partial_value, "frame").astype(jnp.float32).astype(jnp.bfloat16)
    positions = jnp.arange(pixels, dtype=jnp.int32)
    row_pos = (positions // GRID_W).astype(jnp.float32) / (GRID_H - 1)
    col_pos = (positions % GRID_W).astype(jnp.float32) / (GRID_W - 1)
    blk = min(tr_dev, 64)
    blocks = tr_dev // blk
    grouped = queries.reshape(blocks, blk, chan)
    sampled_list, row_list, col_list = ([], [], [])
    maps = feature_maps[0]

    def per_block(qblock):
        return block_terms(qblock, maps, conv_weight, conv_bias, head_weight, row_pos, col_pos)

    sampled_f, row_f, col_f = lax.map(per_block, grouped)
    sampled_list.append(sampled_f.reshape(tr_dev, chan))
    row_list.append(row_f.reshape(tr_dev))
    col_list.append(col_f.reshape(tr_dev))
    sampled = jnp.stack(sampled_list, axis=1)
    row_est = jnp.stack(row_list, axis=1)
    col_est = jnp.stack(col_list, axis=1)
    rims = padded_2(sampled, (("frame", 1),), 1)
    projected = project(rims, mix_in)
    global_frame = frame_here * f_dev - 1 + jnp.arange(f_dev + 2, dtype=jnp.int32)
    valid = (global_frame >= 0) & (global_frame < frame_count * f_dev)
    extended = jnp.where(valid[None, :, None], projected, 0.0)
    delta = temporal_mix(extended, temporal_taps, mix_gain, mix_out)
    local_est = assemble(row_est, col_est, delta).reshape(frame_count, sub_rows, 3, f_dev)
    gathered = lax.all_to_all(local_est, "frame", split_axis=0, concat_axis=3, tiled=True)
    return gathered.reshape(sub_rows, 3, frame_count * f_dev)


def solution(mesh):
    placed = (
        P(("clip", "frame"), None, None),
        P("clip"),
        P("clip"),
        P("clip"),
        P("clip"),
        P(),
        P(),
        P(),
        P(),
        P(),
        P(),
        P(),
    )
    return jax.shard_map(
        on_device,
        mesh=mesh,
        in_specs=placed,
        out_specs=P(("clip", "frame", "track"), None, None),
        check_vma=False,
    )
```

profile of v0, /device:TPU:0, one launch (start us, length us, event | category | flops | bytes accessed | tf_op | source)
XLA Modules:
  0.0 402.7 jit_solution(6857952410239867091)
XLA Ops:
  6.8 1.6 gather_fusion
  8.4 1.6 gather_fusion.1
  10.1 1.6 gather_fusion.2
  11.7 1.6 gather_fusion.3
  13.4 2.6 gather_fusion.4
  16.0 0.7 broadcast_select_fusion
  16.8 36.8 %all-reduce.3.cloned.1.call-done = bf16[2,64,256]{2,1,0:T(8,128)(2,1)} async-done(((bf16[2,64,256]{2,1,0:T(8,128)(2,1)}), bf16[2,64,256]{2,1,0:T(8,128)(2,1)}) %all-reduce.3.cloned.1.call-update) | async-done | bytes 65552 | tf_op jit(solution)/shard_map/psum | solution.py:127
  53.6 322.9 %while.17 = (s32[]{:T(128)}, bf16[2,64,256]{2,1,0:T(8,128)(2,1)S(1)}, bf16[2,64]{1,0:T(2,128)(2,1)S(1)}, bf16[2,64]{1,0:T(2,128)(2,1)S(1)}, f32[16]{0:T(128)S(1)...) while((s32[]{:T(128)}, ...), condition=%wide.region_6.7_spmd.clone, body=%wide.region_1.6_spmd.clone.sunk | while | flops 359751424 | bytes 14882489 | solution.py:140
  53.6 0.7 fusion.90
  54.3 0.7 fusion.91
  55.1 0.7 fusion.92
  55.8 0.7 fusion.93
  56.5 0.7 fusion.94
  57.2 0.7 fusion.95
  58.0 0.7 fusion.87
  58.7 0.7 fusion.96
  59.4 0.7 fusion.88
  60.1 0.7 fusion.89
  60.8 2.4 convolution_multiply_fusion.2
  63.2 2.2 reshape.346
  65.4 142.6 %fusion.97 = (f32[64]{0:T(128)S(1)}, f32[64,64,64]{2,1,0:T(8,128)S(1)}) fusion(f32[]{:T(128)} %bitcast.408, f32[]{:T(128)} %bitcast.409, f32[]{:T(128)} %bitcast.410, f32[]{:T(128)} %bitcast.411, f32[64,64,64]{2,1,0:T(8,128)} %reshape.346, f32[]{:T(128)} %bitcast.412, f32[]{:T(128)} %bitcast.413, f32[]{:T(128)} %bitcast.414, f32[]{:T(128)} %bitcast.415, ...), kind=kLoop, calls=%fused_computation.97.clone.1 | loop fusion | flops 88080320 | bytes 2098112 | tf_op jit(solution)/shard_map/while/body/eval_jaxpr/reduce_max | solution.py:49
  208.0 1.0 fusion.98
  209.1 1.8 multiply_reduce_fusion.4
  211.0 1.6 reshape.347
  212.6 2.4 fusion.99
  215.1 0.7 fusion.90
  215.8 0.7 fusion.91
  216.5 0.7 fusion.92
  217.3 0.7 fusion.93
  218.0 0.7 fusion.94
  218.7 0.7 fusion.95
  219.4 0.7 fusion.87
  220.1 0.7 fusion.96
  220.8 0.7 fusion.88
  221.6 0.7 fusion.89
  222.3 2.4 convolution_multiply_fusion.2
  224.6 2.2 reshape.346
  226.8 142.6 %fusion.97 = (f32[64]{0:T(128)S(1)}, f32[64,64,64]{2,1,0:T(8,128)S(1)}) fusion(f32[]{:T(128)} %bitcast.408, f32[]{:T(128)} %bitcast.409, f32[]{:T(128)} %bitcast.410, f32[]{:T(128)} %bitcast.411, f32[64,64,64]{2,1,0:T(8,128)} %reshape.346, f32[]{:T(128)} %bitcast.412, f32[]{:T(128)} %bitcast.413, f32[]{:T(128)} %bitcast.414, f32[]{:T(128)} %bitcast.415, ...), kind=kLoop, calls=%fused_computation.97.clone.1 | loop fusion | flops 88080320 | bytes 2098112 | tf_op jit(solution)/shard_map/while/body/eval_jaxpr/reduce_max | solution.py:49
  369.4 1.0 fusion.98
  370.6 1.8 multiply_reduce_fusion.4
  372.4 1.6 reshape.347
  374.1 2.4 fusion.99
  376.5 3.3 collective-permute-start
  379.8 1.3 collective-permute-start.1
  381.3 0.4 collective-permute-done
  381.7 4.3 %collective-permute-done.1 = bf16[128,1,256]{2,0,1:T(8,128)(2,1)S(1)} collective-permute-done((bf16[128,1,256]{2,0,1:T(8,128)(2,1)S(1)}, bf16[128,1,256]{2,0,1:T(8,128)(2,1)S(1)}, u32[]{:S(2)}, u32[]{:S(2)}) %collective-permute-start.1) | collective-permute-done | bytes 65568 | tf_op jit(solution)/shard_map/ppermute | solution.py:20
  387.3 7.9 %all_to_all.15 = f32[4,32,3,1]{1,3,2,0:T(1,128)S(1)} all-to-all(f32[4,32,3,1]{1,3,2,0:T(1,128)S(1)} %copy.15), channel_id=1, replica_groups=mesh['clip'=2,'frame'=4,'track'=4] {'frame'}, dimensions={0} | all-to-all | bytes 3072 | tf_op jit(solution)/shard_map/all_to_all | solution.py:154
  395.2 0.6 copy.18
  (55 shorter events, 2.2 us)
Async XLA Ops:
  6.5 379.5 %copy-start = (bf16[256,1024]{1,0:T(8,128)(2,1)S(1)}, bf16[256,1024]{1,0:T(8,128)(2,1)}, u32[]{:S(2)}) copy-start(bf16[256,1024]{1,0:T(8,128)(2,1)} %param.22) | copy-start | bytes 1572868
  6.5 10.2 %copy-start.4 = (f32[3,1024]{1,0:T(4,128)S(1)}, f32[3,1024]{1,0:T(4,128)}, u32[]{:S(2)}) copy-start(f32[3,1024]{1,0:T(4,128)} %param.23) | copy-start | bytes 36868
  6.5 47.1 %copy-start.1 = (f32[16,9]{1,0:T(8,128)S(1)}, f32[16,9]{1,0:T(8,128)}, u32[]{:S(2)}) copy-start(f32[16,9]{1,0:T(8,128)} %param.19) | copy-start | bytes 1732
  6.5 47.1 %copy-start.3 = (f32[16]{0:T(128)S(1)}, f32[16]{0:T(128)}, u32[]{:S(2)}) copy-start(f32[16]{0:T(128)} %param.20) | copy-start | bytes 196
  6.5 47.1 %copy-start.2 = (f32[16]{0:T(128)S(1)}, f32[16]{0:T(128)}, u32[]{:S(2)}) copy-start(f32[16]{0:T(128)} %param.21) | copy-start | bytes 196
  6.5 47.0 %all-reduce.3.cloned.1.call-start = ((), (), s32[]{:S(2)}) async-start(), calls=%async_computation.1 | async-start | bytes 131072 | tf_op jit(solution)/shard_map/psum | solution.py:127
  376.5 5.2 %collective-permute-start = (bf16[128,1,256]{2,0,1:T(8,128)(2,1)S(1)}, bf16[128,1,256]{2,0,1:T(8,128)(2,1)S(1)}, u32[]{:S(2)}, u32[]{:S(2)}) collective-permute-start(bf16[128,1,256]{2,0,1:T(8,128)(2,1)S(1)} %bitcast.589), channel_id=1, source_target_pairs={{0,4},{4,8},{8,12},{1,5},{5,9},{9,13},{2,6},{6,10},{10,14},{3,7},{... | collective-permute-start | bytes 196616 | tf_op jit(solution)/shard_map/ppermute | solution.py:17
  379.8 6.2 %collective-permute-start.1 = (bf16[128,1,256]{2,0,1:T(8,128)(2,1)S(1)}, bf16[128,1,256]{2,0,1:T(8,128)(2,1)S(1)}, u32[]{:S(2)}, u32[]{:S(2)}) collective-permute-start(bf16[128,1,256]{2,0,1:T(8,128)(2,1)S(1)} %bitcast.590), channel_id=1, source_target_pairs={{4,0},{8,4},{12,8},{5,1},{9,5},{13,9},{6,2},{10,6},{14,10},{7,3},{... | collective-permute-start | bytes 196616 | tf_op jit(solution)/shard_map/ppermute | solution.py:20
  381.3 5.3 %copy-start.5 = (bf16[1024,3]{0,1:T(4,128)(2,1)S(1)}, bf16[1024,3]{0,1:T(4,128)(2,1)}, u32[]{:S(2)}) copy-start(bf16[1024,3]{0,1:T(4,128)(2,1)} %param.25) | copy-start | bytes 18436
  381.3 5.3 %copy-start.6 = (f32[1024]{0:T(1024)S(1)}, f32[1024]{0:T(1024)}, u32[]{:S(2)}) copy-start(f32[1024]{0:T(1024)} %param.24) | copy-start | bytes 12292
Sparse Core Ops, SparseCore 0:
  16.9 36.6 all-reduce.2
where the time goes:
time: 406 us; the launch traced here: 403 us
  other arithmetic  292 us (72%)
  waiting for transfers between devices  41.5 us (10%)
  local copies, waits for them, and re-layouts  32.8 us (8%)
  between operations  13.5 us (3%)
  matrix products  10.4 us (3%)
  blocking collectives  7.93 us (2%)
  starting transfers between devices  4.65 us (1%)
    reduce_max x2, other arithmetic, block_terms(): heat = jax.nn.softmax(logit.reshape(cost.shape), axis=-1)  285 us
    psum x1, waiting for transfers between devices, on_device(): lax.psum(partial_value, 'frame').astype(jnp.float32).astype(jnp.bfloat16)  36.8 us
    slice x16, local copies, waits for them, and re-layouts, conv_logits(): conv_weight[channel, tap]  11.5 us
  transfers between devices with their start and end apart: 3, of which 3 were waited for; matrix products, arithmetic and copies ran while one was open for 0% of the time, Pallas kernels for 0%

commit v1 on v0

v1 whole, which is shorter than its diff:
```python
import functools
import math

import jax
import jax.numpy as jnp
from jax import lax
from jax.experimental import pallas as pl
from jax.experimental.pallas import tpu as pltpu
from jax.sharding import PartitionSpec as P

GRID_H = 64
GRID_W = 64
MESH = pl.DeviceIdType.MESH
LANES = 128
F32 = jnp.float32
BF16 = jnp.bfloat16


def kernel(
    dims,
    *refs,
):
    count = 12
    sources = refs[:count]
    out_ref = refs[count]
    held = refs[count + 1 : 2 * count + 1]
    (
        maps_ref,
        frame_ref,
        row_ref,
        col_ref,
        order_ref,
        weight_ref,
        bias_ref,
        head_ref,
        mix_in_ref,
        taps_ref,
        gain_ref,
        mix_out_ref,
    ) = held
    (
        qpart,
        qrecv,
        xs,
        bands,
        logit,
        ssend,
        srecv,
        qsend_sem,
        qrecv_sem,
        ssend_sem,
        srecv_sem,
        load_sem,
        maps_sem,
    ) = refs[2 * count + 1 :]
    frames, tracks, sub, group, wire = dims
    stages = frames // group
    rows = group * sub
    pixels, chan = maps_ref.shape
    total = order_ref.shape[1]
    slots_here = frames * sub
    hid = weight_ref.shape[0]
    tiles = pixels // LANES
    me = lax.axis_index("frame")
    track_here = lax.axis_index("track")

    barrier = pltpu.get_barrier_semaphore()
    for off in range(1, frames):
        pl.semaphore_signal(
            barrier, inc=1, device_id={"frame": lax.rem(me + off, frames)}, device_id_type=MESH
        )

    pieces = maps_sem.shape[0]
    piece = pixels // pieces
    loads = {}
    for i in (1, 2, 3, 4):
        loads[i] = pltpu.make_async_copy(sources[i], held[i], load_sem.at[i])
        loads[i].start()
    maps_loads = []
    for i in range(pieces):
        part = pl.ds(i * piece, piece)
        copy = pltpu.make_async_copy(sources[0].at[part], maps_ref.at[part], maps_sem.at[i])
        copy.start()
        maps_loads.append(copy)
    for i in (5, 6, 7, 8, 9, 10, 11):
        loads[i] = pltpu.make_async_copy(sources[i], held[i], load_sem.at[i])
        loads[i].start()
    for i in (1, 2, 3, 4):
        loads[i].wait()

    code = (frame_ref[...] * pixels + row_ref[...] * GRID_W + col_ref[...]).astype(F32)
    order = order_ref[...].astype(F32)
    slot = lax.broadcasted_iota(jnp.int32, (slots_here, 1), 0)
    slot = ((slot // sub) * tracks + track_here) * sub + slot % sub
    lane = lax.broadcasted_iota(jnp.int32, (slots_here, total), 1)
    picked = jnp.sum(jnp.where(lane == slot, order, 0.0), axis=1, keepdims=True)
    picked = picked.astype(jnp.int32)
    place = jnp.sum(jnp.where(lane == picked, code, 0.0), axis=1, keepdims=True)
    place = place.astype(jnp.int32) - me * pixels

    step = 512
    owned = jnp.zeros((slots_here, chan), F32)
    lane = lax.broadcasted_iota(jnp.int32, (slots_here, step), 1)
    for start in range(0, pixels, step):
        if start % piece == 0:
            maps_loads[start // piece].wait()
        hot = jnp.where(lane == place - start, 1.0, 0.0).astype(BF16)
        owned = owned + jnp.dot(hot, maps_ref[start : start + step, :], preferred_element_type=F32)
    owned = owned.astype(wire).reshape(frames, sub, chan)
    qpart[0:frames] = owned
    qpart[frames : 2 * frames] = owned

    pl.semaphore_wait(barrier, frames - 1)
    sends = []
    for st in range(stages):
        for off in range(1, frames):
            dest = lax.rem(me + off, frames)
            copy = pltpu.make_async_remote_copy(
                src_ref=qpart.at[pl.ds(lax.rem(dest + 1 + group * st, frames), group)],
                dst_ref=qrecv.at[off - 1, st],
                send_sem=qsend_sem.at[off - 1, st],
                recv_sem=qrecv_sem.at[off - 1, st],
                device_id={"frame": dest},
                device_id_type=MESH,
            )
            copy.start()
            sends.append(copy)

    k = lax.broadcasted_iota(jnp.int32, (2 * LANES, LANES), 0)
    n = lax.broadcasted_iota(jnp.int32, (2 * LANES, LANES), 1)
    down = k // GRID_W - n // GRID_W
    along = k % GRID_W - n % GRID_W + 1
    inside = (down >= 0) & (down < 3) & (along >= 0) & (along < 3)
    tap = jnp.where(inside, 3 * down + along, -1)
    for i in (5, 6, 7):
        loads[i].wait()
    span = 2 * LANES
    for h in range(hid):
        band = jnp.zeros((span, LANES), F32)
        for j in range(9):
            band = jnp.where(tap == j, weight_ref[h : h + 1, j : j + 1], band)
        high = band.astype(BF16)
        at = slice((h % 2) * LANES, (h % 2 + 1) * LANES)
        bands[h // 2, 0:span, at] = high
        bands[h // 2, span : 2 * span, at] = high
        bands[h // 2, 2 * span : 3 * span, at] = (band - high.astype(F32)).astype(BF16)

    for base in (0, span):
        xs[0:rows, base : base + GRID_W] = jnp.zeros((rows, GRID_W), BF16)
        xs[(tiles - 1) * rows : tiles * rows, base + LANES + GRID_W : base + span] = jnp.zeros(
            (rows, GRID_W), BF16
        )
    heads = [head_ref[0:1, h : h + 1] for h in range(hid)]
    floors = [-bias_ref[0:1, h : h + 1] for h in range(hid)]

    lane = lax.broadcasted_iota(jnp.int32, (rows, LANES), 1)
    low = (lane // GRID_W).astype(F32)
    colpos = (lane % GRID_W).astype(F32)
    scale = 1.0 / math.sqrt(chan)

    for st in range(stages):
        q = qpart[pl.ds(lax.rem(me + 1 + group * st, frames), group)].astype(F32)
        for off in range(1, frames):
            sends[st * (frames - 1) + off - 1].wait_recv()
            q = q + qrecv[off - 1, st].astype(F32)
        q = (q.reshape(rows, chan) * scale).astype(BF16)

        for i in range(0, tiles + 1, 2):
            first = max(LANES * i - GRID_W, 0)
            last = min(LANES * (i + 2) - GRID_W, pixels)
            cost = lax.dot_general(
                q, maps_ref[first:last, :], (((1,), (1,)), ((), ())), preferred_element_type=F32
            )
            high = cost.astype(BF16)
            rest = (cost - high.astype(F32)).astype(BF16)
            for base, value in ((0, high), (span, rest)):
                if i == 0:
                    xs[0:rows, base + GRID_W : base + LANES] = value[:, :GRID_W]
                    second = value[:, GRID_W : GRID_W + LANES]
                elif i == tiles:
                    xs[(i - 1) * rows : i * rows, base + LANES : base + LANES + GRID_W] = value
                    continue
                else:
                    xs[i * rows : (i + 1) * rows, base : base + LANES] = value[:, :LANES]
                    xs[(i - 1) * rows : i * rows, base + LANES : base + span] = value[:, :LANES]
                    second = value[:, LANES:]
                xs[i * rows : (i + 1) * rows, base + LANES : base + span] = second
                xs[(i + 1) * rows : (i + 2) * rows, base : base + LANES] = second

        chunk = min(256, tiles * rows)
        for start in range(0, tiles * rows, chunk):
            here = slice(start, start + chunk)
            left = jnp.concatenate([xs[here, :], xs[here, 0:span]], axis=1)
            total_here = jnp.zeros((chunk, LANES), F32)
            for h in range(0, hid, 2):
                y = jnp.dot(left, bands[h // 2], preferred_element_type=F32)
                total_here = total_here + heads[h] * jnp.maximum(y[:, :LANES], floors[h])
                total_here = total_here + heads[h + 1] * jnp.maximum(y[:, LANES:], floors[h + 1])
            logit[here, :] = total_here

        top = logit[0:rows, :]
        for i in range(1, tiles):
            top = jnp.maximum(top, logit[i * rows : (i + 1) * rows, :])
        top = jnp.max(top, axis=1, keepdims=True)
        mass = jnp.zeros((rows, LANES), F32)
        height = jnp.zeros((rows, LANES), F32)
        for i in range(tiles):
            e = jnp.exp(logit[i * rows : (i + 1) * rows, :] - top)
            logit[i * rows : (i + 1) * rows, :] = e
            mass = mass + e
            height = height + (2.0 * i) * e
        inv = 1.0 / jnp.sum(mass, axis=1, keepdims=True)
        row_est = jnp.sum(height + low * mass, axis=1, keepdims=True) * inv * (1.0 / (GRID_H - 1))
        col_est = jnp.sum(colpos * mass, axis=1, keepdims=True) * inv * (1.0 / (GRID_W - 1))
        sampled = jnp.zeros((rows, chan), F32)
        for i in range(0, tiles, 2):
            heat = jnp.concatenate(
                [
                    logit[i * rows : (i + 1) * rows, :] * inv,
                    logit[(i + 1) * rows : (i + 2) * rows, :] * inv,
                ],
                axis=1,
            ).astype(BF16)
            sampled = sampled + jnp.dot(
                heat, maps_ref[i * LANES : (i + 2) * LANES, :], preferred_element_type=F32
            )
        extra = jnp.where(lane == 0, row_est, jnp.where(lane == 1, col_est, 0.0))
        message = jnp.concatenate([sampled, extra], axis=1).astype(BF16).astype(wire)
        message = message.reshape(group, sub, chan + LANES)
        for g in range(group):
            j = st * group + g
            if j == frames - 1:
                srecv[me] = message[g]
            else:
                ssend[j] = message[g]
                copy = pltpu.make_async_remote_copy(
                    src_ref=ssend.at[j],
                    dst_ref=srecv.at[me],
                    send_sem=ssend_sem.at[j],
                    recv_sem=srecv_sem.at[j],
                    device_id={"frame": lax.rem(me + 1 + j, frames)},
                    device_id_type=MESH,
                )
                copy.start()
                sends.append(copy)

    for j in range(frames - 1):
        sends[stages * (frames - 1) + j].wait_recv()

    for i in (8, 9, 10, 11):
        loads[i].wait()
    got = srecv[...].astype(BF16) if wire != BF16 else srecv[...]
    rowcol = got[:, :, chan : chan + LANES].astype(F32)
    z = jnp.dot(
        got[:, :, :chan].reshape(slots_here, chan), mix_in_ref[...], preferred_element_type=F32
    )
    hidden = []
    for t in range(frames):
        mixed = taps_ref[1:2, :] * z[t * sub : (t + 1) * sub]
        if t > 0:
            mixed = taps_ref[0:1, :] * z[(t - 1) * sub : t * sub] + mixed
        if t < frames - 1:
            mixed = mixed + taps_ref[2:3, :] * z[(t + 1) * sub : (t + 2) * sub]
        mean = jnp.mean(mixed * mixed, axis=1, keepdims=True)
        normed = mixed * lax.rsqrt(mean + 1e-06) * gain_ref[...]
        hidden.append(jax.nn.gelu(normed).astype(BF16))
    delta = lax.dot_general(
        mix_out_ref[...],
        jnp.concatenate(hidden, axis=0),
        (((1,), (1,)), ((), ())),
        preferred_element_type=F32,
    )
    estimate = delta + rowcol.reshape(slots_here, LANES).T[0:3, :]
    for t in range(frames):
        for c in range(3):
            out_ref[c, t : t + 1, :] = estimate[c : c + 1, t * sub : (t + 1) * sub]

    for copy in sends:
        copy.wait_send()


def on_device(
    feature_maps,
    query_frame,
    query_row,
    query_col,
    track_order,
    conv_weight,
    conv_bias,
    head_weight,
    mix_in,
    temporal_taps,
    mix_gain,
    mix_out,
):
    frames = lax.axis_size("frame")
    tracks = lax.axis_size("track")
    _, pixels, chan = feature_maps.shape
    total = track_order.shape[0]
    sub = total // (tracks * frames)
    hid = conv_weight.shape[0]
    mixw = mix_in.shape[1]
    wire = BF16 if sub % 16 == 0 else F32
    group = max(1, min(frames, 64 // sub))
    while frames % group:
        group -= 1
    stages = frames // group
    rows = group * sub
    tiles = pixels // LANES
    dma = pltpu.SemaphoreType.DMA
    args = (
        feature_maps.reshape(pixels, chan),
        query_frame.reshape(1, total),
        query_row.reshape(1, total),
        query_col.reshape(1, total),
        track_order.reshape(1, total),
        conv_weight,
        conv_bias.reshape(1, hid),
        head_weight.reshape(1, hid),
        mix_in,
        temporal_taps,
        mix_gain.reshape(1, mixw),
        mix_out.T,
    )
    out = pl.pallas_call(
        functools.partial(kernel, (frames, tracks, sub, group, wire)),
        out_shape=jax.ShapeDtypeStruct((3, frames, sub), F32),
        in_specs=[pl.BlockSpec(memory_space=pl.ANY)] * len(args),
        out_specs=pl.BlockSpec(memory_space=pltpu.VMEM),
        scratch_shapes=[pltpu.VMEM(x.shape, x.dtype) for x in args]
        + [
            pltpu.VMEM((2 * frames, sub, chan), wire),
            pltpu.VMEM((frames - 1, stages, group, sub, chan), wire),
            pltpu.VMEM((tiles * rows, 4 * LANES), BF16),
            pltpu.VMEM((hid // 2, 6 * LANES, 2 * LANES), BF16),
            pltpu.VMEM((tiles * rows, LANES), F32),
            pltpu.VMEM((frames - 1, sub, chan + LANES), wire),
            pltpu.VMEM((frames, sub, chan + LANES), wire),
            dma((frames - 1, stages)),
            dma((frames - 1, stages)),
            dma((frames - 1,)),
            dma((frames - 1,)),
            dma((len(args),)),
            dma((4,)),
        ],
        compiler_params=pltpu.CompilerParams(
            collective_id=0, has_side_effects=True, vmem_limit_bytes=62 * 1024 * 1024
        ),
    )(*args)
    return out.transpose(2, 0, 1)


def solution(mesh):
    placed = (
        P(("clip", "frame"), None, None),
        P("clip"),
        P("clip"),
        P("clip"),
        P("clip"),
        P(),
        P(),
        P(),
        P(),
        P(),
        P(),
        P(),
    )
    return jax.shard_map(
        on_device,
        mesh=mesh,
        in_specs=placed,
        out_specs=P(("clip", "frame", "track"), None, None),
        check_vma=False,
    )
```

time: 406 us -> 34.3 us (0.08)
  other arithmetic: 292 us -> 0 us
  waiting for transfers between devices: 41.5 us -> 0 us
  Pallas kernels: 0 us -> 32.8 us
  local copies, waits for them, and re-layouts: 32.8 us -> 1.29 us
  between operations: 13.5 us -> 0.01 us
  matrix products: 10.4 us -> 0 us
  blocking collectives: 7.93 us -> 0 us
  starting transfers between devices: 4.65 us -> 0 us
    reduce_max x2 -> x0, other arithmetic: 285 us -> none  [block_terms(): heat = jax.nn.softmax(logit.reshape(cost.shape), axis=-1)]
    psum x1 -> x0, waiting for transfers between devices: 36.8 us -> none  [on_device(): lax.psum(partial_value, 'frame').astype(jnp.float32).astype(jnp.bfloat16)]
    pallas_call x0 -> x1, Pallas kernels: none -> 32.8 us  [on_device(): pl.pallas_call(functools.partial(kernel, (frames, tracks, sub, group, wir...]
    slice x21 -> x0, local copies, waits for them, and re-layouts: 14.4 us -> none  [the longest x16 11.5 us: conv_logits(): conv_weight[channel, tap]]
    dot_general x6 -> x0, matrix products: 10.4 us -> none  [the longest x2 4.86 us: block_terms(): jnp.dot(heat.astype(jnp.bfloat16), maps, preferred_element_type=jnp.float32)]
    gather x5 -> x0, local copies, waits for them, and re-layouts: 9.19 us -> none  [the longest x2 3.29 us: on_device(): pixel_ids = query_row[tracks] * GRID_W + query_col[tracks]]
    all_to_all x1 -> x0, blocking collectives: 7.93 us -> none  [on_device(): lax.all_to_all(local_est, 'frame', split_axis=0, concat_axis=3, tiled=True)]
    reshape x4 -> x0, local copies, waits for them, and re-layouts: 7.63 us -> none  [the longest x2 4.37 us: block_terms(): cost.reshape(cost.shape[0], GRID_H, GRID_W)]
  transfers between devices with their start and end apart: 3 -> 0, of which waited for: 3 -> 0; matrix products, arithmetic and copies ran while one was open for 0% -> 0% of each run, Pallas kernels for 0% -> 0%
where the time goes in v1:
time: 34.3 us; the launch traced here: 34.1 us
  Pallas kernels  32.8 us (96%)
  local copies, waits for them, and re-layouts  1.29 us (4%)
    pallas_call x1, Pallas kernels, on_device(): pl.pallas_call(functools.partial(kernel, (frames, tracks, sub, group, wir...  32.8 us
    unnamed x1, local copies, waits for them, and re-layouts  1.29 us

profile of v1, /device:TPU:0, one launch (start us, length us, event | category | flops | bytes accessed | tf_op | source)
XLA Modules:
  0.0 34.1 jit_solution(3177128142854465699)
XLA Ops:
  0.0 32.8 %shard_map.118 = f32[3,4,32]{2,1,0:T(4,128)} custom-call(bf16[4096,256]{1,0:T(8,128)(2,1)} %bitcast.10, s32[1,512]{1,0:T(1,128)} %bitcast.14, s32[1,512]{1,0:T(1,128)} %bitcast.15, s32[1,512]{1,0:T(1,128)} %bitcast.16, s32[1,512]{1,0:T(1,128)} %bitcast.17, f32[16,9]{1,0:T(8,128)} %refs_5_.1, f32[1,16]{1,0:T(1,128)} %bitcast.18, f32[1,16]{1,0:T(1,128)} %bitcast.19, ...), custom_call_target="tpu_custom_call" | custom-call | tf_op jit(solution)/shard_map/pallas_call | solution.py:325
  32.8 1.3 %copy.14 = f32[32,3,4]{0,2,1:T(4,128)} copy(f32[32,3,4]{0,2,1:T(4,128)} %bitcast.11) | data formatting | bytes 3072

commit v2 on v1

--- a/solution.py
+++ b/solution.py
@@ -14,6 +14,7 @@
 LANES = 128
 F32 = jnp.float32
 BF16 = jnp.bfloat16
+F8 = jnp.float8_e5m2
 
 
 def kernel(
@@ -42,7 +43,9 @@
         qpart,
         qrecv,
         xs,
+        xs8,
         bands,
+        bands8,
         logit,
         ssend,
         srecv,
@@ -141,15 +144,14 @@
             band = jnp.where(tap == j, weight_ref[h : h + 1, j : j + 1], band)
         high = band.astype(BF16)
         at = slice((h % 2) * LANES, (h % 2 + 1) * LANES)
-        bands[h // 2, 0:span, at] = high
-        bands[h // 2, span : 2 * span, at] = high
-        bands[h // 2, 2 * span : 3 * span, at] = (band - high.astype(F32)).astype(BF16)
-
-    for base in (0, span):
-        xs[0:rows, base : base + GRID_W] = jnp.zeros((rows, GRID_W), BF16)
-        xs[(tiles - 1) * rows : tiles * rows, base + LANES + GRID_W : base + span] = jnp.zeros(
-            (rows, GRID_W), BF16
-        )
+        bands[h // 2, :, at] = high
+        bands8[h // 2, 0:span, at] = band.astype(F8)
+        bands8[h // 2, span : 2 * span, at] = (band - high.astype(F32)).astype(F8)
+
+    for held_in, base in ((xs, 0), (xs8, 0), (xs8, span)):
+        blank = jnp.zeros((rows, GRID_W), held_in.dtype)
+        held_in[0:rows, base : base + GRID_W] = blank
+        held_in[(tiles - 1) * rows : tiles * rows, base + LANES + GRID_W : base + span] = blank
     heads = [head_ref[0:1, h : h + 1] for h in range(hid)]
     floors = [-bias_ref[0:1, h : h + 1] for h in range(hid)]
 
@@ -172,28 +174,30 @@
                 q, maps_ref[first:last, :], (((1,), (1,)), ((), ())), preferred_element_type=F32
             )
             high = cost.astype(BF16)
-            rest = (cost - high.astype(F32)).astype(BF16)
-            for base, value in ((0, high), (span, rest)):
+            rest = (cost - high.astype(F32)).astype(F8)
+            for out, base, value in ((xs, 0, high), (xs8, 0, rest), (xs8, span, cost.astype(F8))):
                 if i == 0:
-                    xs[0:rows, base + GRID_W : base + LANES] = value[:, :GRID_W]
+                    out[0:rows, base + GRID_W : base + LANES] = value[:, :GRID_W]
                     second = value[:, GRID_W : GRID_W + LANES]
                 elif i == tiles:
-                    xs[(i - 1) * rows : i * rows, base + LANES : base + LANES + GRID_W] = value
+                    out[(i - 1) * rows : i * rows, base + LANES : base + LANES + GRID_W] = value
                     continue
                 else:
-                    xs[i * rows : (i + 1) * rows, base : base + LANES] = value[:, :LANES]
-                    xs[(i - 1) * rows : i * rows, base + LANES : base + span] = value[:, :LANES]
+                    out[i * rows : (i + 1) * rows, base : base + LANES] = value[:, :LANES]
+                    out[(i - 1) * rows : i * rows, base + LANES : base + span] = value[:, :LANES]
                     second = value[:, LANES:]
-                xs[i * rows : (i + 1) * rows, base + LANES : base + span] = second
-                xs[(i + 1) * rows : (i + 2) * rows, base : base + LANES] = second
+                out[i * rows : (i + 1) * rows, base + LANES : base + span] = second
+                out[(i + 1) * rows : (i + 2) * rows, base : base + LANES] = second
 
         chunk = min(256, tiles * rows)
         for start in range(0, tiles * rows, chunk):
             here = slice(start, start + chunk)
-            left = jnp.concatenate([xs[here, :], xs[here, 0:span]], axis=1)
+            left = xs[here, :]
+            left8 = xs8[here, :]
             total_here = jnp.zeros((chunk, LANES), F32)
             for h in range(0, hid, 2):
                 y = jnp.dot(left, bands[h // 2], preferred_element_type=F32)
+                y = y + jnp.dot(left8, bands8[h // 2], preferred_element_type=F32)
                 total_here = total_here + heads[h] * jnp.maximum(y[:, :LANES], floors[h])
                 total_here = total_here + heads[h + 1] * jnp.maximum(y[:, LANES:], floors[h + 1])
             logit[here, :] = total_here
@@ -331,8 +335,10 @@
         + [
             pltpu.VMEM((2 * frames, sub, chan), wire),
             pltpu.VMEM((frames - 1, stages, group, sub, chan), wire),
-            pltpu.VMEM((tiles * rows, 4 * LANES), BF16),
-            pltpu.VMEM((hid // 2, 6 * LANES, 2 * LANES), BF16),
+            pltpu.VMEM((tiles * rows, 2 * LANES), BF16),
+            pltpu.VMEM((tiles * rows, 4 * LANES), F8),
+            pltpu.VMEM((hid // 2, 2 * LANES, 2 * LANES), BF16),
+            pltpu.VMEM((hid // 2, 4 * LANES, 2 * LANES), F8),
             pltpu.VMEM((tiles * rows, LANES), F32),
             pltpu.VMEM((frames - 1, sub, chan + LANES), wire),
             pltpu.VMEM((frames, sub, chan + LANES), wire),

time: 34.3 us -> 30.2 us (0.88)
  Pallas kernels: 32.8 us -> 28.7 us
    pallas_call x1, Pallas kernels: 32.8 us -> 28.7 us  [on_device(): pl.pallas_call(functools.partial(kernel, (frames, tracks, sub, group, wir...]
where the time goes in v2:
time: 30.2 us; the launch traced here: 30 us
  Pallas kernels  28.7 us (95%)
  local copies, waits for them, and re-layouts  1.29 us (4%)
    pallas_call x1, Pallas kernels, on_device(): pl.pallas_call(functools.partial(kernel, (frames, tracks, sub, group, wir...  28.7 us
    unnamed x1, local copies, waits for them, and re-layouts  1.29 us

profile of v2, /device:TPU:0, one launch (start us, length us, event | category | flops | bytes accessed | tf_op | source)
XLA Modules:
  0.0 30.0 jit_solution(8963851875014074401)
XLA Ops:
  0.0 28.7 %shard_map.118 = f32[3,4,32]{2,1,0:T(4,128)} custom-call(bf16[4096,256]{1,0:T(8,128)(2,1)} %bitcast.10, s32[1,512]{1,0:T(1,128)} %bitcast.14, s32[1,512]{1,0:T(1,128)} %bitcast.15, s32[1,512]{1,0:T(1,128)} %bitcast.16, s32[1,512]{1,0:T(1,128)} %bitcast.17, f32[16,9]{1,0:T(8,128)} %refs_5_.1, f32[1,16]{1,0:T(1,128)} %bitcast.18, f32[1,16]{1,0:T(1,128)} %bitcast.19, ...), custom_call_target="tpu_custom_call" | custom-call | tf_op jit(solution)/shard_map/pallas_call | solution.py:329
  28.7 1.3 %copy.14 = f32[32,3,4]{0,2,1:T(4,128)} copy(f32[32,3,4]{0,2,1:T(4,128)} %bitcast.11) | data formatting | bytes 3072

commit v3 on v2

--- a/solution.py
+++ b/solution.py
@@ -56,9 +56,7 @@
         load_sem,
         maps_sem,
     ) = refs[2 * count + 1 :]
-    frames, tracks, sub, group, wire = dims
-    stages = frames // group
-    rows = group * sub
+    frames, tracks, sub, stages, wire = dims
     pixels, chan = maps_ref.shape
     total = order_ref.shape[1]
     slots_here = frames * sub
@@ -114,20 +112,24 @@
     qpart[frames : 2 * frames] = owned
 
     pl.semaphore_wait(barrier, frames - 1)
-    sends = []
-    for st in range(stages):
+    queries = []
+    for st, (begin, group) in enumerate(stages):
+        copies = []
         for off in range(1, frames):
             dest = lax.rem(me + off, frames)
-            copy = pltpu.make_async_remote_copy(
-                src_ref=qpart.at[pl.ds(lax.rem(dest + 1 + group * st, frames), group)],
-                dst_ref=qrecv.at[off - 1, st],
-                send_sem=qsend_sem.at[off - 1, st],
-                recv_sem=qrecv_sem.at[off - 1, st],
-                device_id={"frame": dest},
-                device_id_type=MESH,
+            copies.append(
+                pltpu.make_async_remote_copy(
+                    src_ref=qpart.at[pl.ds(lax.rem(dest + 1 + begin, frames), group)],
+                    dst_ref=qrecv.at[off - 1, pl.ds(begin, group)],
+                    send_sem=qsend_sem.at[off - 1, st],
+                    recv_sem=qrecv_sem.at[off - 1, st],
+                    device_id={"frame": dest},
+                    device_id_type=MESH,
+                )
             )
-            copy.start()
-            sends.append(copy)
+        queries.append(copies)
+    for copy in queries[0]:
+        copy.start()
 
     k = lax.broadcasted_iota(jnp.int32, (2 * LANES, LANES), 0)
     n = lax.broadcasted_iota(jnp.int32, (2 * LANES, LANES), 1)
@@ -148,24 +150,33 @@
         bands8[h // 2, 0:span, at] = band.astype(F8)
         bands8[h // 2, span : 2 * span, at] = (band - high.astype(F32)).astype(F8)
 
-    for held_in, base in ((xs, 0), (xs8, 0), (xs8, span)):
-        blank = jnp.zeros((rows, GRID_W), held_in.dtype)
-        held_in[0:rows, base : base + GRID_W] = blank
-        held_in[(tiles - 1) * rows : tiles * rows, base + LANES + GRID_W : base + span] = blank
     heads = [head_ref[0:1, h : h + 1] for h in range(hid)]
     floors = [-bias_ref[0:1, h : h + 1] for h in range(hid)]
 
-    lane = lax.broadcasted_iota(jnp.int32, (rows, LANES), 1)
-    low = (lane // GRID_W).astype(F32)
-    colpos = (lane % GRID_W).astype(F32)
     scale = 1.0 / math.sqrt(chan)
 
-    for st in range(stages):
-        q = qpart[pl.ds(lax.rem(me + 1 + group * st, frames), group)].astype(F32)
+    for copies in queries[1:2]:
+        for copy in copies:
+            copy.start()
+    sends = []
+
+    for st, (begin, group) in enumerate(stages):
+        rows = group * sub
+        lane = lax.broadcasted_iota(jnp.int32, (rows, LANES), 1)
+        low = (lane // GRID_W).astype(F32)
+        colpos = (lane % GRID_W).astype(F32)
+        for held_in, base in ((xs, 0), (xs8, 0), (xs8, span)):
+            blank = jnp.zeros((rows, GRID_W), held_in.dtype)
+            held_in[0:rows, base : base + GRID_W] = blank
+            held_in[(tiles - 1) * rows : tiles * rows, base + LANES + GRID_W : base + span] = blank
+        q = qpart[pl.ds(lax.rem(me + 1 + begin, frames), group)].astype(F32)
         for off in range(1, frames):
-            sends[st * (frames - 1) + off - 1].wait_recv()
-            q = q + qrecv[off - 1, st].astype(F32)
+            queries[st][off - 1].wait_recv()
+            q = q + qrecv[off - 1, begin : begin + group].astype(F32)
         q = (q.reshape(rows, chan) * scale).astype(BF16)
+        for copies in queries[st + 2 : st + 3]:
+            for copy in copies:
+                copy.start()
 
         for i in range(0, tiles + 1, 2):
             first = max(LANES * i - GRID_W, 0)
@@ -232,7 +243,7 @@
         message = jnp.concatenate([sampled, extra], axis=1).astype(BF16).astype(wire)
         message = message.reshape(group, sub, chan + LANES)
         for g in range(group):
-            j = st * group + g
+            j = begin + g
             if j == frames - 1:
                 srecv[me] = message[g]
             else:
@@ -249,7 +260,7 @@
                 sends.append(copy)
 
     for j in range(frames - 1):
-        sends[stages * (frames - 1) + j].wait_recv()
+        sends[j].wait_recv()
 
     for i in (8, 9, 10, 11):
         loads[i].wait()
@@ -279,7 +290,7 @@
         for c in range(3):
             out_ref[c, t : t + 1, :] = estimate[c : c + 1, t * sub : (t + 1) * sub]
 
-    for copy in sends:
+    for copy in [copy for copies in queries for copy in copies] + sends:
         copy.wait_send()
 
 
@@ -305,11 +316,10 @@
     hid = conv_weight.shape[0]
     mixw = mix_in.shape[1]
     wire = BF16 if sub % 16 == 0 else F32
-    group = max(1, min(frames, 64 // sub))
-    while frames % group:
-        group -= 1
-    stages = frames // group
-    rows = group * sub
+    unit = max(1, min(frames, 32 // sub))
+    cuts = sorted({0, unit, max(unit, frames - unit), frames})
+    stages = [(begin, end - begin) for begin, end in zip(cuts, cuts[1:])]
+    rows = sub * max(group for _, group in stages)
     tiles = pixels // LANES
     dma = pltpu.SemaphoreType.DMA
     args = (
@@ -327,14 +337,14 @@
         mix_out.T,
     )
     out = pl.pallas_call(
-        functools.partial(kernel, (frames, tracks, sub, group, wire)),
+        functools.partial(kernel, (frames, tracks, sub, stages, wire)),
         out_shape=jax.ShapeDtypeStruct((3, frames, sub), F32),
         in_specs=[pl.BlockSpec(memory_space=pl.ANY)] * len(args),
         out_specs=pl.BlockSpec(memory_space=pltpu.VMEM),
         scratch_shapes=[pltpu.VMEM(x.shape, x.dtype) for x in args]
         + [
             pltpu.VMEM((2 * frames, sub, chan), wire),
-            pltpu.VMEM((frames - 1, stages, group, sub, chan), wire),
+            pltpu.VMEM((frames - 1, frames, sub, chan), wire),
             pltpu.VMEM((tiles * rows, 2 * LANES), BF16),
             pltpu.VMEM((tiles * rows, 4 * LANES), F8),
             pltpu.VMEM((hid // 2, 2 * LANES, 2 * LANES), BF16),
@@ -342,15 +352,15 @@
             pltpu.VMEM((tiles * rows, LANES), F32),
             pltpu.VMEM((frames - 1, sub, chan + LANES), wire),
             pltpu.VMEM((frames, sub, chan + LANES), wire),
-            dma((frames - 1, stages)),
-            dma((frames - 1, stages)),
+            dma((frames - 1, len(stages))),
+            dma((frames - 1, len(stages))),
             dma((frames - 1,)),
             dma((frames - 1,)),
             dma((len(args),)),
             dma((4,)),
         ],
         compiler_params=pltpu.CompilerParams(
-            collective_id=0, has_side_effects=True, vmem_limit_bytes=62 * 1024 * 1024
+            collective_id=0, has_side_effects=True, vmem_limit_bytes=56 * 1024 * 1024
         ),
     )(*args)
     return out.transpose(2, 0, 1)

time: 30.2 us -> 26.8 us (0.89)
  Pallas kernels: 28.7 us -> 25.3 us
    pallas_call x1, Pallas kernels: 28.7 us -> 25.3 us  [on_device(): pl.pallas_call(functools.partial(kernel, (frames, tracks, sub, stages, wi...]
where the time goes in v3:
time: 26.8 us; the launch traced here: 26.6 us
  Pallas kernels  25.3 us (94%)
  local copies, waits for them, and re-layouts  1.29 us (5%)
    pallas_call x1, Pallas kernels, on_device(): pl.pallas_call(functools.partial(kernel, (frames, tracks, sub, stages, wi...  25.3 us
    unnamed x1, local copies, waits for them, and re-layouts  1.29 us

profile of v3, /device:TPU:0, one launch (start us, length us, event | category | flops | bytes accessed | tf_op | source)
XLA Modules:
  0.0 26.6 jit_solution(13788239201889757370)
XLA Ops:
  0.0 25.3 %shard_map.118 = f32[3,4,32]{2,1,0:T(4,128)} custom-call(bf16[4096,256]{1,0:T(8,128)(2,1)} %bitcast.10, s32[1,512]{1,0:T(1,128)} %bitcast.14, s32[1,512]{1,0:T(1,128)} %bitcast.15, s32[1,512]{1,0:T(1,128)} %bitcast.16, s32[1,512]{1,0:T(1,128)} %bitcast.17, f32[16,9]{1,0:T(8,128)} %refs_5_.1, f32[1,16]{1,0:T(1,128)} %bitcast.18, f32[1,16]{1,0:T(1,128)} %bitcast.19, ...), custom_call_target="tpu_custom_call" | custom-call | tf_op jit(solution)/shard_map/pallas_call | solution.py:339
  25.3 1.3 %copy.14 = f32[32,3,4]{0,2,1:T(4,128)} copy(f32[32,3,4]{0,2,1:T(4,128)} %bitcast.11) | data formatting | bytes 3072

commit v4 on v3

--- a/solution.py
+++ b/solution.py
@@ -42,11 +42,11 @@
     (
         qpart,
         qrecv,
-        xs,
-        xs8,
+        xs_all,
+        xs8_all,
         bands,
         bands8,
-        logit,
+        logit_all,
         ssend,
         srecv,
         qsend_sem,
@@ -160,11 +160,10 @@
             copy.start()
     sends = []
 
-    for st, (begin, group) in enumerate(stages):
+    def prepare(st):
+        begin, group = stages[st]
         rows = group * sub
-        lane = lax.broadcasted_iota(jnp.int32, (rows, LANES), 1)
-        low = (lane // GRID_W).astype(F32)
-        colpos = (lane % GRID_W).astype(F32)
+        xs, xs8 = xs_all.at[st % 2], xs8_all.at[st % 2]
         for held_in, base in ((xs, 0), (xs8, 0), (xs8, span)):
             blank = jnp.zeros((rows, GRID_W), held_in.dtype)
             held_in[0:rows, base : base + GRID_W] = blank
@@ -200,6 +199,13 @@
                 out[i * rows : (i + 1) * rows, base + LANES : base + span] = second
                 out[(i + 1) * rows : (i + 2) * rows, base : base + LANES] = second
 
+    prepare(0)
+    for st, (begin, group) in enumerate(stages):
+        rows = group * sub
+        xs, xs8, logit = xs_all.at[st % 2], xs8_all.at[st % 2], logit_all.at[st % 2]
+        lane = lax.broadcasted_iota(jnp.int32, (rows, LANES), 1)
+        low = (lane // GRID_W).astype(F32)
+        colpos = (lane % GRID_W).astype(F32)
         chunk = min(256, tiles * rows)
         for start in range(0, tiles * rows, chunk):
             here = slice(start, start + chunk)
@@ -212,6 +218,9 @@
                 total_here = total_here + heads[h] * jnp.maximum(y[:, :LANES], floors[h])
                 total_here = total_here + heads[h + 1] * jnp.maximum(y[:, LANES:], floors[h + 1])
             logit[here, :] = total_here
+
+        if st + 1 < len(stages):
+            prepare(st + 1)
 
         top = logit[0:rows, :]
         for i in range(1, tiles):
@@ -338,18 +347,18 @@
     )
     out = pl.pallas_call(
         functools.partial(kernel, (frames, tracks, sub, stages, wire)),
-        out_shape=jax.ShapeDtypeStruct((3, frames, sub), F32),
+        out_shape=pltpu.VMEM((3, frames, sub), F32),
         in_specs=[pl.BlockSpec(memory_space=pl.ANY)] * len(args),
         out_specs=pl.BlockSpec(memory_space=pltpu.VMEM),
         scratch_shapes=[pltpu.VMEM(x.shape, x.dtype) for x in args]
         + [
             pltpu.VMEM((2 * frames, sub, chan), wire),
             pltpu.VMEM((frames - 1, frames, sub, chan), wire),
-            pltpu.VMEM((tiles * rows, 2 * LANES), BF16),
-            pltpu.VMEM((tiles * rows, 4 * LANES), F8),
+            pltpu.VMEM((2, tiles * rows, 2 * LANES), BF16),
+            pltpu.VMEM((2, tiles * rows, 4 * LANES), F8),
             pltpu.VMEM((hid // 2, 2 * LANES, 2 * LANES), BF16),
             pltpu.VMEM((hid // 2, 4 * LANES, 2 * LANES), F8),
-            pltpu.VMEM((tiles * rows, LANES), F32),
+            pltpu.VMEM((2, tiles * rows, LANES), F32),
             pltpu.VMEM((frames - 1, sub, chan + LANES), wire),
             pltpu.VMEM((frames, sub, chan + LANES), wire),
             dma((frames - 1, len(stages))),

time: 26.8 us -> 25.2 us (0.940)
  Pallas kernels: 25.3 us -> 24.4 us
  local copies, waits for them, and re-layouts: 1.29 us -> 0.6 us
    pallas_call x1, Pallas kernels: 25.3 us -> 24.4 us  [on_device(): pl.pallas_call(functools.partial(kernel, (frames, tracks, sub, stages, wi...]
    unnamed x1, local copies, waits for them, and re-layouts: 1.29 us -> 0.6 us
where the time goes in v4:
time: 25.2 us; the launch traced here: 25.1 us
  Pallas kernels  24.4 us (97%)
  local copies, waits for them, and re-layouts  0.6 us (2%)
    pallas_call x1, Pallas kernels, on_device(): pl.pallas_call(functools.partial(kernel, (frames, tracks, sub, stages, wi...  24.4 us
    unnamed x1, local copies, waits for them, and re-layouts  0.6 us

profile of v4, /device:TPU:0, one launch (start us, length us, event | category | flops | bytes accessed | tf_op | source)
XLA Modules:
  0.0 25.1 jit_solution(14581525163380290688)
XLA Ops:
  0.0 24.4 %shard_map.118 = f32[3,4,32]{2,1,0:T(4,128)S(1)} custom-call(bf16[4096,256]{1,0:T(8,128)(2,1)} %bitcast.11, s32[1,512]{1,0:T(1,128)} %bitcast.14, s32[1,512]{1,0:T(1,128)} %bitcast.15, s32[1,512]{1,0:T(1,128)} %bitcast.16, s32[1,512]{1,0:T(1,128)} %bitcast.17, f32[16,9]{1,0:T(8,128)} %refs_5_.1, f32[1,16]{1,0:T(1,128)} %bitcast.18, f32[1,16]{1,0:T(1,128)} %bitcast.19, ...), custom_call_target="tpu_custom_call" | custom-call | tf_op jit(solution)/shard_map/pallas_call | solution.py:348
  24.5 0.6 %copy.14 = f32[32,3,4]{0,2,1:T(4,128)} copy(f32[32,3,4]{0,2,1:T(4,128)S(1)} %bitcast.10) | data formatting | bytes 3072
